TPU v7x, 32 devices: a whole 2x2x4 slice. The times are simulated.
32 devices in a mesh: sec: 4 (over z), row: 8 (over y, x, core).
Axes of the slice: x: 2, y: 2, z: 4, core: 2. Of those that a mesh axis runs over, the one named last changes fastest.
Arguments:
- image: float32 [16384, 4096], P(('sec', 'row')), parts along dimension 0, may hold values from -6 to 6
- cutoff: int32 [4], P('sec'), parts along dimension 0, may hold values from 512 to 1535
Outputs:
- filtered: float32 [16384, 4096], P(('sec', 'row')), parts along dimension 0
There are 4 independent parts, one for each index of `sec`. A program takes and returns all parts, laid end to end along the dimension named above; each array names one. Nothing has to cross between parts.
All inputs are finite; a program needn't handle non-finite values.
Results may differ from a plain program's by a relative error of at most 0.00007.
Values sent between devices are 32-bit elements; how exact they have to be, the bound alone decides.
A program may use at most 128 MiB of HBM per device.

v0:
```python
import math

import jax
import jax.numpy as jnp
from jax import lax
from jax.sharding import PartitionSpec as P

HIGHEST = lax.Precision.HIGHEST


def factor_pair(length):
    first = 1
    for trial in range(1, math.isqrt(length) + 1):
        if length % trial == 0:
            first = trial
    return (first, length // first)


def dft_table(length, direction):
    steps = jnp.arange(length, dtype=jnp.int32)
    product = steps[:, None] * steps[None, :] % length
    angles = direction * 2.0 * math.pi * product.astype(jnp.float32) / length
    return (jnp.cos(angles), jnp.sin(angles))


def twiddle_table(first, second, direction):
    outer_idx = jnp.arange(first, dtype=jnp.int32)
    inner_idx = jnp.arange(second, dtype=jnp.int32)
    product = outer_idx[:, None] * inner_idx[None, :] % (first * second)
    angles = direction * 2.0 * math.pi * product.astype(jnp.float32) / (first * second)
    return (jnp.cos(angles), jnp.sin(angles))


def rows_dft(real_part, imag_part, direction):
    nrows, length = real_part.shape
    first, second = factor_pair(length)
    first_cos, first_sin = dft_table(first, direction)
    second_cos, second_sin = dft_table(second, direction)
    twid_cos, twid_sin = twiddle_table(first, second, direction)
    real_cube = real_part.reshape(nrows, first, second)
    segment_real = jnp.einsum("ka,ram->rkm", first_cos, real_cube, precision=HIGHEST)
    segment_imag = jnp.einsum("ka,ram->rkm", first_sin, real_cube, precision=HIGHEST)
    if imag_part is not None:
        imag_cube = imag_part.reshape(nrows, first, second)
        segment_real = segment_real - jnp.einsum(
            "ka,ram->rkm", first_sin, imag_cube, precision=HIGHEST
        )
        segment_imag = segment_imag + jnp.einsum(
            "ka,ram->rkm", first_cos, imag_cube, precision=HIGHEST
        )
    turned_real = segment_real * twid_cos - segment_imag * twid_sin
    turned_imag = segment_real * twid_sin + segment_imag * twid_cos
    final_real = jnp.einsum("qm,rkm->rqk", second_cos, turned_real, precision=HIGHEST) - jnp.einsum(
        "qm,rkm->rqk", second_sin, turned_imag, precision=HIGHEST
    )
    final_imag = jnp.einsum("qm,rkm->rqk", second_cos, turned_imag, precision=HIGHEST) + jnp.einsum(
        "qm,rkm->rqk", second_sin, turned_real, precision=HIGHEST
    )
    return (final_real.reshape(nrows, length), final_imag.reshape(nrows, length))


def swap_halves(stacked):
    half_width = stacked.shape[-1] // 2
    return jnp.concatenate([-stacked[..., half_width:], stacked[..., :half_width]], axis=-1)


def stacked_multiply(stacked, factor_cos, factor_sin):
    half_width = stacked.shape[-1] // 2
    real_part = stacked[..., :half_width]
    imag_part = stacked[..., half_width:]
    return jnp.concatenate(
        [
            real_part * factor_cos - imag_part * factor_sin,
            real_part * factor_sin + imag_part * factor_cos,
        ],
        axis=-1,
    )


def columns_dft(stacked, direction):
    length, width = stacked.shape
    first, second = factor_pair(length)
    first_cos, first_sin = dft_table(first, direction)
    second_cos, second_sin = dft_table(second, direction)
    twid_cos, twid_sin = twiddle_table(first, second, direction)
    cube = stacked.reshape(first, second, width)
    segment = jnp.einsum("ka,amw->kmw", first_cos, cube, precision=HIGHEST) + swap_halves(
        jnp.einsum("ka,amw->kmw", first_sin, cube, precision=HIGHEST)
    )
    segment = stacked_multiply(segment, twid_cos[:, :, None], twid_sin[:, :, None])
    final = jnp.einsum("qm,kmw->qkw", second_cos, segment, precision=HIGHEST) + swap_halves(
        jnp.einsum("qm,kmw->qkw", second_sin, segment, precision=HIGHEST)
    )
    return final.reshape(length, width)


def folded(indices, total):
    return jnp.minimum(indices, total - indices)


def body(image, cutoff):
    rows_local, width = image.shape
    shards = lax.axis_size("row")
    position = lax.axis_index("row")
    height = rows_local * shards
    row_real, row_imag = rows_dft(image, None, -1.0)
    half_width = width // 2
    send_real = row_real[:, :half_width]
    send_imag = jnp.concatenate(
        [row_real[:, half_width : half_width + 1], row_imag[:, 1:half_width]], axis=1
    )
    columns_local = send_real.shape[1] // shards
    packed = jnp.stack(
        [
            send_real.reshape(rows_local, shards, columns_local),
            send_imag.reshape(rows_local, shards, columns_local),
        ],
        axis=2,
    ).reshape(rows_local, 2 * shards * columns_local)
    column_data = lax.all_to_all(packed, "row", split_axis=1, concat_axis=0, tiled=True)
    column_spec = columns_dft(column_data, -1.0)
    radius = cutoff[0]
    row_freq = folded(jnp.arange(height, dtype=jnp.int32), height)
    col_freq = folded(position * columns_local + jnp.arange(columns_local, dtype=jnp.int32), width)
    passed = (
        row_freq[:, None] * row_freq[:, None] + col_freq[None, :] * col_freq[None, :]
        >= radius * radius
    ).astype(jnp.float32)
    masked = column_spec * jnp.concatenate([passed, passed], axis=1)
    zero_real = column_spec[:, 0]
    zero_imag = column_spec[:, columns_local]
    mirror_real = jnp.roll(jnp.flip(zero_real, 0), 1, 0)
    mirror_imag = jnp.roll(jnp.flip(zero_imag, 0), 1, 0)
    square_rows = row_freq * row_freq
    keep_zero = (square_rows >= radius * radius).astype(jnp.float32)
    nyquist = width // 2
    keep_edge = (square_rows + nyquist * nyquist >= radius * radius).astype(jnp.float32)
    fixed_real = keep_zero * 0.5 * (zero_real + mirror_real) + keep_edge * 0.5 * (
        zero_real - mirror_real
    )
    fixed_imag = keep_zero * 0.5 * (zero_imag - mirror_imag) + keep_edge * 0.5 * (
        zero_imag + mirror_imag
    )
    is_first = position == 0
    masked = masked.at[:, 0].set(jnp.where(is_first, fixed_real, masked[:, 0]))
    masked = masked.at[:, columns_local].set(
        jnp.where(is_first, fixed_imag, masked[:, columns_local])
    )
    column_back = columns_dft(masked, 1.0)
    row_data = lax.all_to_all(column_back, "row", split_axis=0, concat_axis=1, tiled=True)
    arranged = row_data.reshape(rows_local, shards, 2, columns_local)
    back_real = arranged[:, :, 0, :].reshape(rows_local, shards * columns_local)
    back_imag = arranged[:, :, 1, :].reshape(rows_local, shards * columns_local)
    inner_real = back_real[:, 1:]
    inner_imag = back_imag[:, 1:]
    zeros_col = jnp.zeros((rows_local, 1), jnp.float32)
    back_real = jnp.concatenate(
        [back_real[:, 0:1], inner_real, back_imag[:, 0:1], jnp.flip(inner_real, 1)], axis=1
    )
    back_imag = jnp.concatenate(
        [zeros_col, inner_imag, zeros_col, -jnp.flip(inner_imag, 1)], axis=1
    )
    final_real, final_imag = rows_dft(back_real, back_imag, 1.0)
    return final_real / (width * height)


def solution(mesh):
    return jax.shard_map(
        body,
        mesh=mesh,
        in_specs=(P(("sec", "row"), None), P("sec")),
        out_specs=P(("sec", "row"), None),
        check_vma=False,
    )
```

profile of v0, /device:TPU:0, one launch (start us, length us, event | category | flops | bytes accessed | tf_op | source)
XLA Modules:
  0.0 846.9 jit_solution(10881203901262452250)
XLA Ops:
  9.4 17.5 %fusion.38 = f32[64,512,64]{1,0,2:T(8,128)} fusion(f32[512,64,64]{0,2,1:T(8,128)} %bitcast.117), kind=kOutput, calls=%fused_computation.55 | convolution fusion | flops 1610670080 | bytes 16777216 | tf_op jit(solution)/shard_map/ka,ram->rkm/dot_general | solution.py:42
  26.9 21.3 %subtract_bitcast_fusion.1 = (f32[512,64,64]{0,1,2:T(8,128)S(1)}, f32[512,64,64]{0,1,2:T(8,128)}) fusion(f32[64,512,64]{1,0,2:T(8,128)} %fusion.38, f32[64,64]{0,1:T(8,128)S(1)} %copy.115, f32[64,64]{0,1:T(8,128)S(1)} %copy.113, f32[512,64,64]{0,2,1:T(8,128)} %bitcast.118), kind=kOutput, calls=%fused_computation.21 | convolution fusion | flops 1623252992 | bytes 33587200 | tf_op jit(solution)/shard_map/ka,ram->rkm/dot_general | solution.py:41
  48.3 18.2 %fusion.30 = f32[512,64,64]{0,2,1:T(8,128)} fusion(f32[512,64,64]{0,1,2:T(8,128)} %get-tuple-element.34), kind=kOutput, calls=%fused_computation.47 | convolution fusion | flops 1610670080 | bytes 16777216 | tf_op jit(solution)/shard_map/qm,rkm->rqk/dot_general | solution.py:56
  66.5 15.1 %fusion.32 = f32[512,64,64]{0,2,1:T(8,128)S(1)} fusion(f32[512,64,64]{0,1,2:T(8,128)S(1)} %copy-done.3), kind=kOutput, calls=%fused_computation.49 | convolution fusion | flops 1610670080 | bytes 16777216 | tf_op jit(solution)/shard_map/qm,rkm->rqk/dot_general | solution.py:53
  81.6 14.6 %subtract_bitcast_fusion = f32[512,64,64]{0,1,2:T(8,128)} fusion(f32[512,64,64]{0,2,1:T(8,128)S(1)} %fusion.32, f32[512,64,64]{0,1,2:T(8,128)S(1)} %get-tuple-element.33), kind=kOutput, calls=%fused_computation.19 | convolution fusion | flops 1612767232 | bytes 25165824 | tf_op jit(solution)/shard_map/qm,rkm->rqk/dot_general | solution.py:53
  96.2 11.5 %copy.118 = f32[512,64,64]{0,2,1:T(8,128)} copy(f32[512,64,64]{0,1,2:T(8,128)} %subtract_bitcast_fusion) | data formatting | bytes 16777216 | tf_op jit(solution)/shard_map/sub | solution.py:53
  111.0 16.0 %add_bitcast_fusion = f32[512,64,64]{0,1,2:T(8,128)} fusion(f32[512,64,64]{0,2,1:T(8,128)} %fusion.30, f32[512,64,64]{0,1,2:T(8,128)S(1)} %get-tuple-element.33), kind=kOutput, calls=%fused_computation.18 | convolution fusion | flops 1612767232 | bytes 25165824 | tf_op jit(solution)/shard_map/qm,rkm->rqk/dot_general | solution.py:56
  150.6 90.1 %all-to-all-done = f32[512,8,512]{0,2,1:T(8,128)} async-done(((f32[512,8,512]{0,2,1:T(8,128)}), f32[512,8,512]{0,2,1:T(8,128)}, u32[]{:S(2)}, u32[]{:S(2)}) %all-to-all-start) | async-done | bytes 8388640 | tf_op jit(solution)/shard_map/all_to_all | solution.py:120
  240.6 9.1 %copy.124 = f32[8,512,512]{2,1,0:T(8,128)} copy(f32[8,512,512]{1,2,0:T(8,128)} %bitcast.16) | data formatting | bytes 16777216 | tf_op jit(solution)/shard_map/all_to_all | solution.py:120
  249.7 16.8 %fusion.26 = f32[64,64,512]{2,0,1:T(8,128)S(1)} fusion(f32[64,64,512]{2,1,0:T(8,128)} %bitcast.109), kind=kOutput, calls=%fused_computation.43 | convolution fusion | flops 1610670080 | bytes 16777216 | tf_op jit(solution)/shard_map/ka,amw->kmw/dot_general | solution.py:88
  269.9 13.9 %maximum_add_fusion = f32[64,64,512]{2,0,1:T(8,128)S(1)} fusion(f32[64,64,256]{2,0,1:T(8,128)} %get-tuple-element.50, f32[64,64,256]{2,0,1:T(8,128)S(1)} %get-tuple-element.49, f32[64,64,512]{2,1,0:T(8,128)S(1)} %bitcast.112), kind=kOutput, calls=%fused_computation.1 | convolution fusion | flops 1614864384 | bytes 25165824 | tf_op jit(solution)/shard_map/ka,amw->kmw/dot_general | solution.py:87
  290.1 13.3 %fusion.22 = f32[64,64,512]{2,0,1:T(8,128)} fusion(f32[64,64,512]{2,0,1:T(8,128)S(1)} %pad_maximum_fusion.1), kind=kOutput, calls=%fused_computation.39 | convolution fusion | flops 1610670080 | bytes 16777216 | tf_op jit(solution)/shard_map/qm,kmw->qkw/dot_general | solution.py:92
  307.6 14.4 %maximum_add_fusion.1 = f32[64,64,512]{2,0,1:T(8,128)} fusion(f32[64,64,256]{2,0,1:T(8,128)S(1)} %get-tuple-element.48, f32[64,64,256]{2,0,1:T(8,128)S(1)} %get-tuple-element.47, f32[64,64,512]{2,0,1:T(8,128)S(1)} %pad_maximum_fusion.1), kind=kOutput, calls=%fused_computation.3 | convolution fusion | flops 1614864384 | bytes 25165824 | tf_op jit(solution)/shard_map/qm,kmw->qkw/dot_general | solution.py:91
  368.1 17.2 %fusion.18 = f32[64,64,512]{2,0,1:T(8,128)S(1)} fusion(f32[64,64,512]{2,1,0:T(8,128)} %bitcast.101), kind=kOutput, calls=%fused_computation.35 | convolution fusion | flops 1610670080 | bytes 16777216 | tf_op jit(solution)/shard_map/ka,amw->kmw/dot_general | solution.py:88
  388.6 13.6 %maximum_add_fusion.2 = f32[64,64,512]{2,0,1:T(8,128)S(1)} fusion(f32[64,64,256]{2,0,1:T(8,128)} %get-tuple-element.44, f32[64,64,256]{2,0,1:T(8,128)S(1)} %get-tuple-element.43, f32[64,64,512]{2,1,0:T(8,128)S(1)} %bitcast.104), kind=kOutput, calls=%fused_computation.4 | convolution fusion | flops 1614864384 | bytes 25165824 | tf_op jit(solution)/shard_map/ka,amw->kmw/dot_general | solution.py:87
  408.6 13.4 %fusion.14 = f32[64,64,512]{2,0,1:T(8,128)} fusion(f32[64,64,512]{2,0,1:T(8,128)S(1)} %pad_maximum_fusion.2), kind=kOutput, calls=%fused_computation.31 | convolution fusion | flops 1610670080 | bytes 16777216 | tf_op jit(solution)/shard_map/qm,kmw->qkw/dot_general | solution.py:92
  426.2 14.5 %maximum_add_fusion.3 = f32[64,64,512]{2,0,1:T(8,128)} fusion(f32[64,64,256]{2,0,1:T(8,128)S(1)} %get-tuple-element.42, f32[64,64,256]{2,0,1:T(8,128)S(1)} %get-tuple-element.41, f32[64,64,512]{2,0,1:T(8,128)S(1)} %pad_maximum_fusion.2), kind=kOutput, calls=%fused_computation.6 | convolution fusion | flops 1614864384 | bytes 25165824 | tf_op jit(solution)/shard_map/qm,kmw->qkw/dot_general | solution.py:91
  448.9 97.9 %all_to_all.32 = f32[8,512,512]{2,1,0:T(8,128)} all-to-all(f32[8,512,512]{2,1,0:T(8,128)S(1)} %bitcast.122), channel_id=1, replica_groups=mesh['sec'=4,'row'=8] {'row'}, dimensions={0} | all-to-all | bytes 16777216 | tf_op jit(solution)/shard_map/all_to_all | solution.py:150
  546.8 10.5 %reshape.258 = f32[512,8,2,256]{3,2,0,1:T(2,128)} reshape(f32[512,8,512]{2,0,1:T(8,128)} %bitcast.123) | data formatting | bytes 16777216 | tf_op jit(solution)/shard_map/reshape | solution.py:151
  557.4 11.8 %fusion.211 = (f32[512,8,1,256]{3,2,0,1:T(1,128)}, f32[512,8,1,256]{3,2,0,1:T(1,128)}) fusion(f32[512,8,2,256]{3,2,0,1:T(2,128)} %reshape.258), kind=kLoop, calls=%fused_computation.235 | loop fusion | bytes 16777216 | tf_op jit(solution)/shard_map/slice | solution.py:153
  569.1 10.9 %copy.154 = f32[512,8,1,256]{0,3,1,2:T(8,128)} copy(f32[512,8,1,256]{3,2,0,1:T(1,128)} %get-tuple-element.39) | data formatting | bytes 8388608
  585.4 33.6 %rev.11 = f32[512,2047]{0,1:T(8,128)} reverse(f32[512,2047]{0,1:T(8,128)} %slice.197), dimensions={1} | reverse | bytes 8384512 | tf_op jit(solution)/shard_map/jit(_flip)/rev | solution.py:161
  623.6 24.0 %concatenate.62 = f32[512,4096]{0,1:T(8,128)} concatenate(f32[512,1]{0,1:T(1,128)S(1)} %broadcast_in_dim.2, f32[512,2047]{0,1:T(8,128)} %slice.197, f32[512,1]{0,1:T(1,128)S(1)} %broadcast_in_dim.2, f32[512,2047]{0,1:T(8,128)} %neg.19), dimensions={1} | concatenate | bytes 16777216 | tf_op jit(solution)/shard_map/concatenate | solution.py:160
  647.6 17.9 %fusion.6 = f32[512,64,64]{0,2,1:T(8,128)} fusion(f32[512,64,64]{0,2,1:T(8,128)} %bitcast.113), kind=kOutput, calls=%fused_computation.23 | convolution fusion | flops 1610670080 | bytes 16777216 | tf_op jit(solution)/shard_map/ka,ram->rkm/dot_general | solution.py:48
  665.5 13.6 %fusion.8 = f32[512,64,64]{0,2,1:T(8,128)} fusion(f32[512,64,64]{0,2,1:T(8,128)S(1)} %bitcast.114), kind=kOutput, calls=%fused_computation.25 | convolution fusion | flops 1610670080 | bytes 16777216 | tf_op jit(solution)/shard_map/ka,ram->rkm/dot_general | solution.py:45
  679.1 10.9 %copy.153 = f32[512,8,1,256]{0,3,1,2:T(8,128)} copy(f32[512,8,1,256]{3,2,0,1:T(1,128)} %get-tuple-element.40) | data formatting | bytes 8388608
  694.7 33.8 %rev.10 = f32[512,2047]{0,1:T(8,128)} reverse(f32[512,2047]{0,1:T(8,128)} %slice.196), dimensions={1} | reverse | bytes 8384512 | tf_op jit(solution)/shard_map/jit(_flip)/rev | solution.py:158
  728.5 22.1 %concatenate.61 = f32[512,4096]{0,1:T(8,128)} concatenate(f32[512,2048]{0,1:T(8,128)} %bitcast.120, f32[512,1]{0,1:T(1,128)S(1)} %slice.195, f32[512,2047]{0,1:T(8,128)} %rev.10), dimensions={1} | concatenate | bytes 16777216 | tf_op jit(solution)/shard_map/concatenate | solution.py:157
  750.6 18.0 %fusion.12 = f32[512,64,64]{0,2,1:T(8,128)} fusion(f32[512,64,64]{0,2,1:T(8,128)} %bitcast.115), kind=kOutput, calls=%fused_computation.29 | convolution fusion | flops 1610670080 | bytes 16777216 | tf_op jit(solution)/shard_map/ka,ram->rkm/dot_general | solution.py:41
  768.6 28.4 %fusion = (f32[512,64,64]{0,1,2:T(8,128)}, f32[512,64,64]{0,1,2:T(8,128)}) fusion(f32[64,64]{0,1:T(8,128)S(1)} %copy.137, f32[64,64]{0,1:T(8,128)S(1)} %copy.136, f32[512,64,64]{0,2,1:T(8,128)} %fusion.6, f32[512,64,64]{0,2,1:T(8,128)} %fusion.12, f32[512,64,64]{0,2,1:T(8,128)} %fusion.8, f32[512,64,64]{0,2,1:T(8,128)} %bitcast.116), kind=kOutput, calls=%fused_computation.9 | convolution fusion | flops 1627447296 | bytes 50364416 | tf_op jit(solution)/shard_map/ka,ram->rkm/dot_general | solution.py:42
  797.0 17.6 %fusion.2 = f32[512,64,64]{0,2,1:T(8,128)S(1)} fusion(f32[512,64,64]{0,1,2:T(8,128)} %get-tuple-element.32), kind=kOutput, calls=%fused_computation.13 | convolution fusion | flops 1610670080 | bytes 16777216 | tf_op jit(solution)/shard_map/qm,rkm->rqk/dot_general | solution.py:53
  814.6 15.1 %multiply_bitcast_fusion = f32[512,64,64]{0,1,2:T(8,128)S(1)} fusion(f32[512,64,64]{0,2,1:T(8,128)S(1)} %fusion.2, f32[512,64,64]{0,1,2:T(8,128)S(1)} %copy-done.4), kind=kOutput, calls=%fused_computation.17 | convolution fusion | flops 1614864384 | bytes 25165824 | tf_op jit(solution)/shard_map/qm,rkm->rqk/dot_general | solution.py:53
  (73 shorter events, 149.2 us)
Async XLA Ops:
  48.3 18.2 %copy-start.3 = (f32[512,64,64]{0,1,2:T(8,128)S(1)}, f32[512,64,64]{0,1,2:T(8,128)}, u32[]{:S(2)}) copy-start(f32[512,64,64]{0,1,2:T(8,128)} %get-tuple-element.34) | copy-start | bytes 25165828
  140.7 100.0 %all-to-all-start = ((f32[512,8,512]{0,2,1:T(8,128)}), f32[512,8,512]{0,2,1:T(8,128)}, u32[]{:S(2)}, u32[]{:S(2)}) async-start(f32[512,8,512]{0,2,1:T(8,128)} %bitcast.121), calls=%async_computation | async-start | bytes 16777216 | tf_op jit(solution)/shard_map/all_to_all | solution.py:120
  249.7 19.6 %slice-start.2 = ((s8[8388608]{0:T(1024)(128)(4,1)}), s8[4194304]{0:T(1024)(128)(4,1)S(1)}, s32[]{:S(2)}) async-start(s8[8388608]{0:T(1024)(128)(4,1)} %bitcast.110), calls=%async_computation.4 | async-start | bytes 8388608
  266.6 3.3 slice-start.3
  330.3 3.4 copy-start.1
  339.2 7.5 copy-start.5
  343.5 3.2 copy-start
  368.1 20.1 %slice-start = ((s8[8388608]{0:T(1024)(128)(4,1)}), s8[4194304]{0:T(1024)(128)(4,1)S(1)}, s32[]{:S(2)}) async-start(s8[8388608]{0:T(1024)(128)(4,1)} %bitcast.102), calls=%async_computation.2 | async-start | bytes 8388608
  385.3 3.3 slice-start.1
  647.6 17.9 %copy-start.2 = (f32[512,4096]{0,1:T(8,128)S(1)}, f32[512,4096]{0,1:T(8,128)}, u32[]{:S(2)}) copy-start(f32[512,4096]{0,1:T(8,128)} %concatenate.62) | copy-start | bytes 25165828
  797.0 17.6 %copy-start.4 = (f32[512,64,64]{0,1,2:T(8,128)S(1)}, f32[512,64,64]{0,1,2:T(8,128)}, u32[]{:S(2)}) copy-start(f32[512,64,64]{0,1,2:T(8,128)} %get-tuple-element.31) | copy-start | bytes 25165828
where the time goes:
time: 860 us; the launch traced here: 847 us
  matrix products  330 us (38%)
  local copies, waits for them, and re-layouts  268 us (31%)
  blocking collectives  97.9 us (11%)
  waiting for transfers between devices  90.1 us (10%)
  other arithmetic  53.9 us (6%)
    all_to_all x1, blocking collectives, body(): lax.all_to_all(column_back, 'row', split_axis=0, concat_axis=1, tiled=True)  97.9 us
    all_to_all x1, waiting for transfers between devices, body(): lax.all_to_all(packed, 'row', split_axis=1, concat_axis=0, tiled=True)  90.1 us
    dot_general x2, matrix products, rows_dft(): jnp.einsum('ka,ram->rkm', first_sin, real_cube, precision=HIGHEST)  46 us
    dot_general x2, matrix products, rows_dft(): jnp.einsum('ka,ram->rkm', first_cos, real_cube, precision=HIGHEST)  39.3 us
    unnamed x27, local copies, waits for them, and re-layouts  38.1 us
    dot_general x2, matrix products, columns_dft(): jnp.einsum('ka,amw->kmw', first_sin, cube, precision=HIGHEST)  34 us
    rev x1, local copies, waits for them, and re-layouts, body(): jnp.flip(inner_real, 1)  33.8 us
    rev x1, local copies, waits for them, and re-layouts, body(): jnp.flip(inner_imag, 1)  33.6 us
  transfers between devices with their start and end apart: 1, of which 1 were waited for; matrix products, arithmetic and copies ran while one was open for 0% of the time, Pallas kernels for 0%

commit v1 on v0

v1 whole, which is shorter than its diff:
```python
import functools
import math

import jax
import jax.numpy as jnp
import ml_dtypes
import numpy as np
from jax import lax
from jax.experimental import pallas as pl
from jax.experimental.pallas import tpu as pltpu
from jax.sharding import PartitionSpec as P

RADIX = 16
UNITS = RADIX // 2
VMEM = 56 * 1024 * 1024


def turn(value, cosine, sine):
    real, imag = value
    if abs(sine) < 1e-12:
        return (real, imag) if cosine > 0 else (-real, -imag)
    if abs(cosine) < 1e-12:
        return (-imag, real) if sine > 0 else (imag, -real)
    if abs(abs(cosine) - abs(sine)) < 1e-12:
        first = real - imag if sine * cosine > 0 else real + imag
        second = real + imag if sine * cosine > 0 else imag - real
        return (first * cosine, second * cosine)
    return (real * cosine - imag * sine, real * sine + imag * cosine)


def plus(one, other):
    return (one[0] + other[0], one[1] + other[1])


def minus(one, other):
    return (one[0] - other[0], one[1] - other[1])


def complex_fft(values, sign):
    count = len(values)
    if count == 1:
        return values
    even = complex_fft(values[0::2], sign)
    odd = complex_fft(values[1::2], sign)
    low, high = [], []
    for k in range(count // 2):
        angle = sign * 2.0 * math.pi * k / count
        turned = turn(odd[k], math.cos(angle), math.sin(angle))
        low.append(plus(even[k], turned))
        high.append(minus(even[k], turned))
    return low + high


def real_fft(values):
    count = len(values)
    if count == 2:
        return [(values[0] + values[1], None), (values[0] - values[1], None)]
    even = real_fft(values[0::2])
    odd = real_fft(values[1::2])
    out = [None] * (count // 2 + 1)
    out[0] = (even[0][0] + odd[0][0], None)
    out[count // 2] = (even[0][0] - odd[0][0], None)
    quarter = count // 4
    out[quarter] = (even[quarter][0], -odd[quarter][0])
    for k in range(1, quarter):
        angle = -2.0 * math.pi * k / count
        turned = turn(odd[k], math.cos(angle), math.sin(angle))
        out[k] = plus(even[k], turned)
        lower = minus(even[k], turned)
        out[count // 2 - k] = (lower[0], -lower[1])
    return out


def real_inverse(values, count):
    if count == 2:
        return [values[0][0] + values[1][0], values[0][0] - values[1][0]]
    half, quarter = count // 2, count // 4
    even = [(values[0][0] + values[half][0], None)]
    odd = [(values[0][0] - values[half][0], None)]
    for k in range(1, quarter):
        mirror = (values[half - k][0], -values[half - k][1])
        even.append(plus(values[k], mirror))
        angle = 2.0 * math.pi * k / count
        odd.append(turn(minus(values[k], mirror), math.cos(angle), math.sin(angle)))
    even.append((2.0 * values[quarter][0], None))
    odd.append((-2.0 * values[quarter][1], None))
    even_out, odd_out = real_inverse(even, half), real_inverse(odd, half)
    return [item for pair in zip(even_out, odd_out) for item in pair]


def split(values):
    high = values.astype(jnp.bfloat16)
    return high, (values - high.astype(jnp.float32)).astype(jnp.bfloat16)


def table_halves(table):
    high = table.astype(np.float32).astype(ml_dtypes.bfloat16)
    low = (table - high.astype(np.float64)).astype(np.float32).astype(ml_dtypes.bfloat16)
    return np.stack([high, low])


def product(left, right, dims):
    def one(a, b):
        return lax.dot_general(a, b, dims, preferred_element_type=jnp.float32)

    return one(left[0], right[0]) + (one(left[0], right[1]) + one(left[1], right[0]))


def twiddles(length):
    chunk = length // RADIX
    angle = 2.0 * math.pi * np.outer(np.arange(RADIX), np.arange(chunk)) / length
    return np.stack([np.cos(angle), np.sin(angle)]).astype(np.float32)


def frequency_table(length, band):
    chunk, kept = length // RADIX, band // UNITS
    half = kept // 2
    inner = np.arange(chunk)[:, None]
    angle = 2.0 * math.pi * (inner * np.arange(-half, half)[None, :] % chunk) / chunk
    c, s = np.cos(angle), np.sin(angle)
    forward = np.block([[c, -s], [s, c]])
    inverse = np.concatenate([np.concatenate([c.T, s.T], 1), np.concatenate([-s.T, c.T], 1)], 0)
    angle0 = 2.0 * math.pi * (inner * (RADIX * np.arange(half))[None, :] % length) / length
    angle8 = 2.0 * math.pi * (inner * (UNITS + RADIX * np.arange(half))[None, :] % length) / length
    zero = np.zeros((chunk, half))
    forward0 = np.block(
        [[np.cos(angle0), zero, -np.sin(angle0), zero], [zero, np.cos(angle8), zero, -np.sin(angle8)]]
    )
    weight = np.full((half, 1), 2.0)
    weight[0, 0] = 1.0
    top = np.concatenate([weight * np.cos(angle0).T, zero.T], 1)
    second = np.concatenate([zero.T, 2.0 * np.cos(angle8).T], 1)
    third = np.concatenate([-weight * np.sin(angle0).T, zero.T], 1)
    fourth = np.concatenate([zero.T, -2.0 * np.sin(angle8).T], 1)
    inverse0 = np.concatenate([top, second, third, fourth], 0)
    return forward0, forward, inverse0, inverse


def rows_forward(image_ref, table_ref, tw_ref, out_ref, high_ref, low_ref):
    rows, length = image_ref.shape
    chunk = length // RADIX
    lanes = min(128, chunk)
    sub = 16

    def step(index, carry):
        at = pl.ds(pl.multiple_of(index * sub, sub), sub)
        for start in range(0, chunk, lanes):
            values = [image_ref[at, n * chunk + start : n * chunk + start + lanes] for n in range(RADIX)]
            freqs = real_fft(values)
            for unit in range(UNITS):
                if unit == 0:
                    pair = (freqs[0][0], freqs[UNITS][0])
                else:
                    real, imag = freqs[unit]
                    c = tw_ref[0, unit : unit + 1, start : start + lanes]
                    s = tw_ref[1, unit : unit + 1, start : start + lanes]
                    pair = (real * c + imag * s, imag * c - real * s)
                for part in range(2):
                    high, low = split(pair[part])
                    high_ref[unit, at, part * chunk + start : part * chunk + start + lanes] = high
                    low_ref[unit, at, part * chunk + start : part * chunk + start + lanes] = low
        return carry

    lax.fori_loop(0, rows // sub, step, 0)
    for unit in range(UNITS):
        which = min(unit, 1)
        out_ref[unit] = product(
            (table_ref[which, 0], table_ref[which, 1]),
            (high_ref[unit], low_ref[unit]),
            (((1,), (1,)), ((), ())),
        )


def columns_filter(scalar_ref, data_ref, fx2_ref, fy2_ref, fwd_ref, inv_ref, tw_ref, out_ref, work_ref):
    sources, _, cols, rows = data_ref.shape
    length = sources * rows
    chunk = length // RADIX
    lanes = min(128, chunk, rows)
    sub = 8

    def where_is(n, start):
        source, first = divmod(n * chunk + start, rows)
        return source, slice(first, first + lanes)

    def step_forward(index, carry):
        at = pl.ds(pl.multiple_of(index * sub, sub), sub)
        for start in range(0, chunk, lanes):
            values = []
            for n in range(RADIX):
                source, span = where_is(n, start)
                values.append((data_ref[source, 0, at, span], data_ref[source, 1, at, span]))
            for k, (real, imag) in enumerate(complex_fft(values, -1.0)):
                if k > 0:
                    c = tw_ref[0, k : k + 1, start : start + lanes]
                    s = tw_ref[1, k : k + 1, start : start + lanes]
                    real, imag = real * c + imag * s, imag * c - real * s
                work_ref[k, at, start : start + lanes] = real
                work_ref[k, at, chunk + start : chunk + start + lanes] = imag
        return carry

    lax.fori_loop(0, cols // sub, step_forward, 0)
    radius = scalar_ref[1]
    limit = radius * radius
    fx2 = fx2_ref[0, :, 0:1]
    dims = (((1,), (0,)), ((), ()))
    group = 4
    for k in range(0, RADIX, group):
        values = work_ref[k : k + group].reshape(group * cols, 2 * chunk)
        spectrum = product(split(values), (fwd_ref[0], fwd_ref[1]), dims)
        width = spectrum.shape[1]
        spectrum = spectrum.reshape(group, cols, width)
        fy2 = fy2_ref[k : k + group].reshape(group, 1, width)
        low = jnp.where(fx2[None] + fy2 < limit, spectrum, 0.0).reshape(group * cols, width)
        back = product(split(low), (inv_ref[0], inv_ref[1]), dims)
        work_ref[k : k + group] = back.reshape(group, cols, 2 * chunk)

    def step_inverse(index, carry):
        at = pl.ds(pl.multiple_of(index * sub, sub), sub)
        for start in range(0, chunk, lanes):
            values = []
            for k in range(RADIX):
                real = work_ref[k, at, start : start + lanes]
                imag = work_ref[k, at, chunk + start : chunk + start + lanes]
                if k > 0:
                    c = tw_ref[0, k : k + 1, start : start + lanes]
                    s = tw_ref[1, k : k + 1, start : start + lanes]
                    real, imag = real * c - imag * s, imag * c + real * s
                values.append((real, imag))
            for n, (real, imag) in enumerate(complex_fft(values, 1.0)):
                source, span = where_is(n, start)
                out_ref[source, 0, at, span] = real
                out_ref[source, 1, at, span] = imag
        return carry

    lax.fori_loop(0, cols // sub, step_inverse, 0)


def rows_inverse(data_ref, image_ref, table_ref, tw_ref, out_ref, work_ref):
    rows, length = image_ref.shape
    chunk = length // RADIX
    lanes = min(128, chunk)
    sub = 8
    for unit in range(UNITS):
        which = min(unit, 1)
        work_ref[unit] = product(
            split(data_ref[unit].T), (table_ref[which, 0], table_ref[which, 1]), (((1,), (0,)), ((), ()))
        )

    def step(index, carry):
        at = pl.ds(pl.multiple_of(index * sub, sub), sub)
        for start in range(0, chunk, lanes):
            freqs = [None] * (UNITS + 1)
            for unit in range(UNITS):
                real = work_ref[unit, at, start : start + lanes]
                imag = work_ref[unit, at, chunk + start : chunk + start + lanes]
                if unit == 0:
                    freqs[0], freqs[UNITS] = (real, None), (imag, None)
                else:
                    c = tw_ref[0, unit : unit + 1, start : start + lanes]
                    s = tw_ref[1, unit : unit + 1, start : start + lanes]
                    freqs[unit] = (real * c - imag * s, imag * c + real * s)
            for n, low in enumerate(real_inverse(freqs, RADIX)):
                span = slice(n * chunk + start, n * chunk + start + lanes)
                out_ref[at, span] = image_ref[at, span] - low
        return carry

    lax.fori_loop(0, rows // sub, step, 0)


def whole(shape):
    return pl.BlockSpec(shape, lambda *_: (0,) * len(shape))


def body(image, cutoff):
    rows_local, width = image.shape
    shards = lax.axis_size("row")
    position = lax.axis_index("row")
    height = rows_local * shards
    band = 3 * width // 8
    kept = band // UNITS
    half = kept // 2
    cols = band // shards
    per = shards // UNITS
    chunk = width // RADIX
    forward0, forward, inverse0, inverse = frequency_table(width, band)
    order = np.arange(2 * kept).reshape(2, per, cols).transpose(1, 0, 2).reshape(-1)
    row_forward = np.stack([table_halves(forward0.T[order]), table_halves(forward.T[order])])
    row_inverse = np.stack([table_halves(inverse0[order]), table_halves(inverse[order])])
    col_forward = table_halves(forward)
    col_inverse = table_halves(inverse / (width * height))
    tw = twiddles(width)
    steps = np.arange(-half, half)
    fy = np.arange(RADIX)[:, None] + RADIX * np.concatenate([steps, steps])[None, :]
    fy2 = (fy * fy).astype(np.int32)
    first = np.arange(half)
    fx = np.concatenate(
        [RADIX * first, UNITS + RADIX * first] + [unit + RADIX * steps for unit in range(1, UNITS)]
    )
    fx2 = np.broadcast_to((fx * fx).reshape(shards, cols, 1), (shards, cols, 128)).astype(np.int32)

    params = pltpu.CompilerParams(vmem_limit_bytes=VMEM)
    block = min(256, rows_local)
    spectrum = pl.pallas_call(
        rows_forward,
        grid=(rows_local // block,),
        out_shape=jax.ShapeDtypeStruct((UNITS, 2 * kept, rows_local), jnp.float32),
        in_specs=[
            pl.BlockSpec((block, width), lambda i: (i, 0)),
            whole(row_forward.shape),
            whole(tw.shape),
        ],
        out_specs=pl.BlockSpec((UNITS, 2 * kept, block), lambda i: (0, 0, i)),
        scratch_shapes=[pltpu.VMEM((UNITS, block, 2 * chunk), jnp.bfloat16)] * 2,
        compiler_params=params,
    )(image, row_forward, tw)
    columns = lax.all_to_all(
        spectrum.reshape(shards, 2 * cols, rows_local), "row", split_axis=0, concat_axis=0, tiled=True
    )
    part = math.gcd(cols, 32)
    scalars = jnp.stack([position.astype(jnp.int32), cutoff[0]])
    data_spec = pl.BlockSpec((shards, 2, part, rows_local), lambda i, s: (0, 0, i, 0))
    back = pl.pallas_call(
        columns_filter,
        grid_spec=pltpu.PrefetchScalarGridSpec(
            num_scalar_prefetch=1,
            grid=(cols // part,),
            in_specs=[
                data_spec,
                pl.BlockSpec((1, part, 128), lambda i, s: (s[0], i, 0)),
                whole(fy2.shape),
                whole(col_forward.shape),
                whole(col_inverse.shape),
                whole(tw.shape),
            ],
            out_specs=data_spec,
            scratch_shapes=[pltpu.VMEM((RADIX, part, 2 * chunk), jnp.float32)],
        ),
        out_shape=jax.ShapeDtypeStruct((shards, 2, cols, rows_local), jnp.float32),
        compiler_params=params,
    )(scalars, columns.reshape(shards, 2, cols, rows_local), fx2, fy2, col_forward, col_inverse, tw)
    returned = lax.all_to_all(
        back.reshape(shards, 2 * cols, rows_local), "row", split_axis=0, concat_axis=0, tiled=True
    )
    block = min(128, rows_local)
    return pl.pallas_call(
        rows_inverse,
        grid=(rows_local // block,),
        out_shape=jax.ShapeDtypeStruct((rows_local, width), jnp.float32),
        in_specs=[
            pl.BlockSpec((UNITS, 2 * kept, block), lambda i: (0, 0, i)),
            pl.BlockSpec((block, width), lambda i: (i, 0)),
            whole(row_inverse.shape),
            whole(tw.shape),
        ],
        out_specs=pl.BlockSpec((block, width), lambda i: (i, 0)),
        scratch_shapes=[pltpu.VMEM((UNITS, block, 2 * chunk), jnp.float32)],
        compiler_params=params,
    )(returned.reshape(UNITS, 2 * kept, rows_local), image, row_inverse, tw)


def solution(mesh):
    return jax.shard_map(
        body,
        mesh=mesh,
        in_specs=(P(("sec", "row"), None), P("sec")),
        out_specs=P(("sec", "row"), None),
        check_vma=False,
    )
```

time: 860 us -> 204 us (0.24); the launches traced: 847 us -> 203 us
  matrix products: 330 us -> 0 us
  local copies, waits for them, and re-layouts: 268 us -> 0 us
  other arithmetic: 53.9 us -> 0.65 us
  Pallas kernels: 0 us -> 49.3 us
  blocking collectives: 97.9 us -> 76.9 us
  waiting for transfers between devices: 90.1 us -> 70.6 us
    dot_general x20 -> x0, matrix products: 330 us -> none  [the longest x2 46 us: rows_dft(): jnp.einsum('ka,ram->rkm', first_sin, real_cube, precision=HIGHEST)]
    rev x2 -> x0, local copies, waits for them, and re-layouts: 67.3 us -> none  [the longest x1 33.8 us: body(): jnp.flip(inner_real, 1)]
    concatenate x4 -> x0, local copies, waits for them, and re-layouts: 50.2 us -> none  [the longest x1 24 us: body(): jnp.concatenate([zeros_col, inner_imag, zeros_col, -jnp.flip(inner_imag,...]
    pallas_call x0 -> x3, Pallas kernels: none -> 49.3 us  [the longest x1 21.3 us: body(): pl.pallas_call(columns_filter, grid_spec=pltpu.PrefetchScalarGridSpec(num...]
    unnamed x27 -> x0, local copies, waits for them, and re-layouts: 38.1 us -> none
    slice x9 -> x0, local copies, waits for them, and re-layouts: 27.5 us -> none  [the longest x1 11.8 us: body(): back_imag = arranged[:, :, 1, :].reshape(rows_local, shards * columns_local)]
    add x3 -> x0, local copies, waits for them, and re-layouts: 24.7 us -> none  [the longest x2 16.5 us: columns_dft(): jnp.einsum('qm,kmw->qkw', second_cos, segment, precision=HIGHEST)]
    all_to_all x1, blocking collectives: 97.9 us -> 76.9 us  [body(): lax.all_to_all(back.reshape(shards, 2 * cols, rows_local), 'row', split_a...]
where the time goes in v1:
time: 204 us; the launch traced here: 203 us
  blocking collectives  76.9 us (38%)
  waiting for transfers between devices  70.6 us (35%)
  Pallas kernels  49.3 us (24%)
  starting transfers between devices  5.18 us (3%)
    all_to_all x1, blocking collectives, body(): lax.all_to_all(back.reshape(shards, 2 * cols, rows_local), 'row', split_a...  76.9 us
    all_to_all x1, waiting for transfers between devices, body(): lax.all_to_all(spectrum.reshape(shards, 2 * cols, rows_local), 'row', spl...  70.6 us
    pallas_call x1, Pallas kernels, body(): pl.pallas_call(columns_filter, grid_spec=pltpu.PrefetchScalarGridSpec(num...  21.3 us
    pallas_call x1, Pallas kernels, body(): pl.pallas_call(rows_inverse, grid=(rows_local // block,), out_shape=jax.S...  14.6 us
    pallas_call x1, Pallas kernels, body(): pl.pallas_call(rows_forward, grid=(rows_local // block,), out_shape=jax.S...  13.4 us
    all_to_all x1, starting transfers between devices, body(): lax.all_to_all(spectrum.reshape(shards, 2 * cols, rows_local), 'row', spl...  5.18 us
  transfers between devices with their start and end apart: 1, of which 1 were waited for; matrix products, arithmetic and copies ran while one was open for 0% of the time, Pallas kernels for 0%

profile of v1, /device:TPU:0, one launch (start us, length us, event | category | flops | bytes accessed | tf_op | source)
XLA Modules:
  0.0 203.2 jit_solution(13125521090417711488)
XLA Ops:
  0.0 13.4 %shard_map.91 = f32[8,384,512]{2,1,0:T(8,128)} custom-call(f32[512,4096]{1,0:T(8,128)} %image_ref.3, bf16[2,2,384,512]{3,2,1,0:T(8,128)(2,1)} %constant.18.clone.table_ref, f32[2,16,256]{2,1,0:T(8,128)} %constant.19.clone.tw_ref), custom_call_target="tpu_custom_call" | custom-call | tf_op jit(solution)/shard_map/pallas_call | solution.py:303
  13.4 5.2 %all-to-all-start = ((f32[8,384,512]{2,1,0:T(8,128)}), f32[8,384,512]{2,1,0:T(8,128)}, u32[]{:S(2)}, u32[]{:S(2)}) async-start(f32[8,384,512]{2,1,0:T(8,128)} %shard_map.91), calls=%async_computation | async-start | bytes 12582912 | tf_op jit(solution)/shard_map/all_to_all | solution.py:316
  19.2 0.6 pad_add_fusion.scalar_ref
  19.9 70.6 %all-to-all-done = f32[8,384,512]{2,1,0:T(8,128)} async-done(((f32[8,384,512]{2,1,0:T(8,128)}), f32[8,384,512]{2,1,0:T(8,128)}, u32[]{:S(2)}, u32[]{:S(2)}) %all-to-all-start) | async-done | bytes 6291488 | tf_op jit(solution)/shard_map/all_to_all | solution.py:316
  90.4 21.3 %shard_map.92 = f32[8,2,192,512]{3,2,1,0:T(8,128)} custom-call(s32[2]{0:T(128)} %pad_add_fusion.scalar_ref, f32[8,2,192,512]{3,2,1,0:T(8,128)} %bitcast.1.data_ref, s32[8,192,128]{2,1,0:T(8,128)} %constant.20.clone.fx2_ref, s32[16,384]{1,0:T(8,128)} %constant.21.clone.fy2_ref, bf16[2,512,384]{2,1,0:T(8,128)(2,1)} %constant.22.clone.fwd_ref, ...), custom_call_target="tpu_custom_call" | custom-call | tf_op jit(solution)/shard_map/pallas_call | solution.py:322
  111.7 76.9 %all_to_all.10.data_ref = f32[8,384,512]{2,1,0:T(8,128)} all-to-all(f32[8,384,512]{2,1,0:T(8,128)} %bitcast.3), channel_id=1, replica_groups=mesh['sec'=4,'row'=8] {'row'}, dimensions={0} | all-to-all | bytes 12582912 | tf_op jit(solution)/shard_map/all_to_all | solution.py:341
  188.6 14.6 %shard_map.93 = f32[512,4096]{1,0:T(8,128)} custom-call(f32[8,384,512]{2,1,0:T(8,128)} %all_to_all.10.data_ref, f32[512,4096]{1,0:T(8,128)} %image_ref.3, bf16[2,2,384,512]{3,2,1,0:T(8,128)(2,1)} %constant.24.clone.table_ref, f32[2,16,256]{2,1,0:T(8,128)} %constant.19.clone.tw_ref), custom_call_target="tpu_custom_call" | custom-call | tf_op jit(solution)/shard_map/pallas_call | solution.py:345
Async XLA Ops:
  13.4 77.0 %all-to-all-start = ((f32[8,384,512]{2,1,0:T(8,128)}), f32[8,384,512]{2,1,0:T(8,128)}, u32[]{:S(2)}, u32[]{:S(2)}) async-start(f32[8,384,512]{2,1,0:T(8,128)} %shard_map.91), calls=%async_computation | async-start | bytes 12582912 | tf_op jit(solution)/shard_map/all_to_all | solution.py:316

commit v2 on v1

--- a/solution.py
+++ b/solution.py
@@ -136,7 +136,7 @@
     return forward0, forward, inverse0, inverse
 
 
-def rows_forward(image_ref, table_ref, tw_ref, out_ref, high_ref, low_ref):
+def rows_forward(image_ref, tw_ref, high_ref, low_ref):
     rows, length = image_ref.shape
     chunk = length // RADIX
     lanes = min(128, chunk)
@@ -162,17 +162,10 @@
         return carry
 
     lax.fori_loop(0, rows // sub, step, 0)
-    for unit in range(UNITS):
-        which = min(unit, 1)
-        out_ref[unit] = product(
-            (table_ref[which, 0], table_ref[which, 1]),
-            (high_ref[unit], low_ref[unit]),
-            (((1,), (1,)), ((), ())),
-        )
-
-
-def columns_filter(scalar_ref, data_ref, fx2_ref, fy2_ref, fwd_ref, inv_ref, tw_ref, out_ref, work_ref):
-    sources, _, cols, rows = data_ref.shape
+
+
+def columns_filter(group, position, cutoff_ref, data_ref, fx2_ref, fy2_ref, fwd_ref, inv_ref, tw_ref, out_ref, work_ref):
+    _, sources, _, cols, rows = data_ref.shape
     length = sources * rows
     chunk = length // RADIX
     lanes = min(128, chunk, rows)
@@ -188,7 +181,7 @@
             values = []
             for n in range(RADIX):
                 source, span = where_is(n, start)
-                values.append((data_ref[source, 0, at, span], data_ref[source, 1, at, span]))
+                values.append((data_ref[group, source, 0, at, span], data_ref[group, source, 1, at, span]))
             for k, (real, imag) in enumerate(complex_fft(values, -1.0)):
                 if k > 0:
                     c = tw_ref[0, k : k + 1, start : start + lanes]
@@ -199,20 +192,25 @@
         return carry
 
     lax.fori_loop(0, cols // sub, step_forward, 0)
-    radius = scalar_ref[1]
+    radius = cutoff_ref[0]
     limit = radius * radius
-    fx2 = fx2_ref[0, :, 0:1]
+    fx2 = fx2_ref[position, group, :, 0:1]
     dims = (((1,), (0,)), ((), ()))
-    group = 4
-    for k in range(0, RADIX, group):
-        values = work_ref[k : k + group].reshape(group * cols, 2 * chunk)
+    batch = 4
+
+    def step_matmul(index, carry):
+        span = pl.ds(index * batch, batch)
+        values = work_ref[span].reshape(batch * cols, 2 * chunk)
         spectrum = product(split(values), (fwd_ref[0], fwd_ref[1]), dims)
         width = spectrum.shape[1]
-        spectrum = spectrum.reshape(group, cols, width)
-        fy2 = fy2_ref[k : k + group].reshape(group, 1, width)
-        low = jnp.where(fx2[None] + fy2 < limit, spectrum, 0.0).reshape(group * cols, width)
+        spectrum = spectrum.reshape(batch, cols, width)
+        fy2 = fy2_ref[span]
+        low = jnp.where(fx2[None] + fy2 < limit, spectrum, 0.0).reshape(batch * cols, width)
         back = product(split(low), (inv_ref[0], inv_ref[1]), dims)
-        work_ref[k : k + group] = back.reshape(group, cols, 2 * chunk)
+        work_ref[span] = back.reshape(batch, cols, 2 * chunk)
+        return carry
+
+    lax.fori_loop(0, RADIX // batch, step_matmul, 0)
 
     def step_inverse(index, carry):
         at = pl.ds(pl.multiple_of(index * sub, sub), sub)
@@ -228,11 +226,104 @@
                 values.append((real, imag))
             for n, (real, imag) in enumerate(complex_fft(values, 1.0)):
                 source, span = where_is(n, start)
-                out_ref[source, 0, at, span] = real
-                out_ref[source, 1, at, span] = imag
+                out_ref[group, source, 0, at, span] = real
+                out_ref[group, source, 1, at, span] = imag
         return carry
 
     lax.fori_loop(0, cols // sub, step_inverse, 0)
+
+
+def exchange(
+    shards, cutoff_ref, image_ref, row_ref, tw_ref, fx2_ref, fy2_ref, fwd_ref, inv_ref, out_ref,
+    high_ref, low_ref, sent_ref, held_ref, work_ref, back_ref, send_sem, recv_sem, back_send, back_recv, own_sem,
+):
+    groups, _, _, cols, rows = held_ref.shape
+    per = shards // UNITS
+    me = lax.axis_index("row")
+
+    def partner(step):
+        return lax.rem(me + step, shards)
+
+    def forward_copy(group, step):
+        dest = partner(step)
+        return pltpu.make_async_remote_copy(
+            src_ref=sent_ref.at[step, group],
+            dst_ref=held_ref.at[group, me],
+            send_sem=send_sem.at[group, step],
+            recv_sem=recv_sem.at[group, step],
+            device_id={"row": dest},
+            device_id_type=pl.DeviceIdType.MESH,
+        )
+
+    def back_copy(group, step):
+        dest = partner(step)
+        return pltpu.make_async_remote_copy(
+            src_ref=back_ref.at[group, dest],
+            dst_ref=out_ref.at[me, group],
+            send_sem=back_send.at[group, step],
+            recv_sem=back_recv.at[group, step],
+            device_id={"row": dest},
+            device_id_type=pl.DeviceIdType.MESH,
+        )
+
+    def own_copy(group):
+        return pltpu.make_async_copy(back_ref.at[group, me], out_ref.at[me, group], own_sem.at[group])
+
+    def every(function):
+        def loop(step, carry):
+            function(step)
+            return carry
+
+        lax.fori_loop(1, shards, loop, 0)
+
+    barrier = pltpu.get_barrier_semaphore()
+    every(
+        lambda step: pl.semaphore_signal(
+            barrier, inc=1, device_id={"row": partner(step)}, device_id_type=pl.DeviceIdType.MESH
+        )
+    )
+    rows_forward(image_ref, tw_ref, high_ref, low_ref)
+    pl.semaphore_wait(barrier, shards - 1)
+
+    def columns_of(dest):
+        unit, part = dest // per, lax.rem(dest, per)
+        which = jnp.minimum(unit, 1)
+        values = product(
+            (row_ref[which, 0, part], row_ref[which, 1, part]),
+            (high_ref[unit], low_ref[unit]),
+            (((1,), (1,)), ((), ())),
+        )
+        return values.reshape(groups, 2, cols, rows)
+
+    def produce(step):
+        sent_ref[step] = columns_of(partner(step))
+        forward_copy(0, step).start()
+
+    every(produce)
+    for group in range(1, groups):
+        every(lambda step: forward_copy(group, step).start())
+    own = columns_of(me)
+    for group in range(groups):
+        held_ref[group, me] = own[group]
+
+    def filter_group(group, carry):
+        every(lambda step: forward_copy(group, step).wait_recv())
+        columns_filter(
+            group, me, cutoff_ref, held_ref, fx2_ref, fy2_ref, fwd_ref, inv_ref, tw_ref, back_ref, work_ref
+        )
+        every(lambda step: back_copy(group, step).start())
+        own_copy(group).start()
+        return carry
+
+    lax.fori_loop(0, groups, filter_group, 0)
+
+    def finish(group, carry):
+        every(lambda step: forward_copy(group, step).wait_send())
+        every(lambda step: back_copy(group, step).wait())
+        own_copy(group).wait()
+        return carry
+
+    lax.fori_loop(0, groups, finish, 0)
 
 
 def rows_inverse(data_ref, image_ref, table_ref, tw_ref, out_ref, work_ref):
@@ -274,7 +365,6 @@
 def body(image, cutoff):
     rows_local, width = image.shape
     shards = lax.axis_size("row")
-    position = lax.axis_index("row")
     height = rows_local * shards
     band = 3 * width // 8
     kept = band // UNITS
@@ -283,64 +373,48 @@
     per = shards // UNITS
     chunk = width // RADIX
     forward0, forward, inverse0, inverse = frequency_table(width, band)
-    order = np.arange(2 * kept).reshape(2, per, cols).transpose(1, 0, 2).reshape(-1)
+    part = math.gcd(cols, 64)
+    groups = cols // part
+    order = np.arange(2 * kept).reshape(2, per, groups, part).transpose(1, 2, 0, 3).reshape(-1)
     row_forward = np.stack([table_halves(forward0.T[order]), table_halves(forward.T[order])])
+    row_forward = row_forward.reshape(2, 2, per, 2 * cols, 2 * chunk)
     row_inverse = np.stack([table_halves(inverse0[order]), table_halves(inverse[order])])
     col_forward = table_halves(forward)
     col_inverse = table_halves(inverse / (width * height))
     tw = twiddles(width)
     steps = np.arange(-half, half)
     fy = np.arange(RADIX)[:, None] + RADIX * np.concatenate([steps, steps])[None, :]
-    fy2 = (fy * fy).astype(np.int32)
+    fy2 = (fy * fy).astype(np.int32)[:, None, :]
     first = np.arange(half)
     fx = np.concatenate(
         [RADIX * first, UNITS + RADIX * first] + [unit + RADIX * steps for unit in range(1, UNITS)]
     )
-    fx2 = np.broadcast_to((fx * fx).reshape(shards, cols, 1), (shards, cols, 128)).astype(np.int32)
-
+    fx2 = np.broadcast_to((fx * fx).reshape(shards, groups, part, 1), (shards, groups, part, 128)).astype(np.int32)
+
+    vmem = pl.BlockSpec(memory_space=pltpu.VMEM)
+    returned = pl.pallas_call(
+        functools.partial(exchange, shards),
+        out_shape=jax.ShapeDtypeStruct((shards, groups, 2, part, rows_local), jnp.float32),
+        in_specs=[pl.BlockSpec(memory_space=pltpu.SMEM)] + [vmem] * 7,
+        out_specs=pl.BlockSpec(memory_space=pl.ANY),
+        scratch_shapes=[
+            pltpu.VMEM((UNITS, rows_local, 2 * chunk), jnp.bfloat16),
+            pltpu.VMEM((UNITS, rows_local, 2 * chunk), jnp.bfloat16),
+            pltpu.VMEM((shards, groups, 2, part, rows_local), jnp.float32),
+            pltpu.VMEM((groups, shards, 2, part, rows_local), jnp.float32),
+            pltpu.VMEM((RADIX, part, 2 * chunk), jnp.float32),
+            pltpu.VMEM((groups, shards, 2, part, rows_local), jnp.float32),
+            pltpu.SemaphoreType.DMA((groups, shards)),
+            pltpu.SemaphoreType.DMA((groups, shards)),
+            pltpu.SemaphoreType.DMA((groups, shards)),
+            pltpu.SemaphoreType.DMA((groups, shards)),
+            pltpu.SemaphoreType.DMA((groups,)),
+        ],
+        compiler_params=pltpu.CompilerParams(
+            vmem_limit_bytes=VMEM, collective_id=0, has_side_effects=True
+        ),
+    )(cutoff, image, row_forward, tw, fx2, fy2, col_forward, col_inverse)
     params = pltpu.CompilerParams(vmem_limit_bytes=VMEM)
-    block = min(256, rows_local)
-    spectrum = pl.pallas_call(
-        rows_forward,
-        grid=(rows_local // block,),
-        out_shape=jax.ShapeDtypeStruct((UNITS, 2 * kept, rows_local), jnp.float32),
-        in_specs=[
-            pl.BlockSpec((block, width), lambda i: (i, 0)),
-            whole(row_forward.shape),
-            whole(tw.shape),
-        ],
-        out_specs=pl.BlockSpec((UNITS, 2 * kept, block), lambda i: (0, 0, i)),
-        scratch_shapes=[pltpu.VMEM((UNITS, block, 2 * chunk), jnp.bfloat16)] * 2,
-        compiler_params=params,
-    )(image, row_forward, tw)
-    columns = lax.all_to_all(
-        spectrum.reshape(shards, 2 * cols, rows_local), "row", split_axis=0, concat_axis=0, tiled=True
-    )
-    part = math.gcd(cols, 32)
-    scalars = jnp.stack([position.astype(jnp.int32), cutoff[0]])
-    data_spec = pl.BlockSpec((shards, 2, part, rows_local), lambda i, s: (0, 0, i, 0))
-    back = pl.pallas_call(
-        columns_filter,
-        grid_spec=pltpu.PrefetchScalarGridSpec(
-            num_scalar_prefetch=1,
-            grid=(cols // part,),
-            in_specs=[
-                data_spec,
-                pl.BlockSpec((1, part, 128), lambda i, s: (s[0], i, 0)),
-                whole(fy2.shape),
-                whole(col_forward.shape),
-                whole(col_inverse.shape),
-                whole(tw.shape),
-            ],
-            out_specs=data_spec,
-            scratch_shapes=[pltpu.VMEM((RADIX, part, 2 * chunk), jnp.float32)],
-        ),
-        out_shape=jax.ShapeDtypeStruct((shards, 2, cols, rows_local), jnp.float32),
-        compiler_params=params,
-    )(scalars, columns.reshape(shards, 2, cols, rows_local), fx2, fy2, col_forward, col_inverse, tw)
-    returned = lax.all_to_all(
-        back.reshape(shards, 2 * cols, rows_local), "row", split_axis=0, concat_axis=0, tiled=True
-    )
     block = min(128, rows_local)
     return pl.pallas_call(
         rows_inverse,

time: 204 us -> 164 us (0.80)
  Pallas kernels: 49.3 us -> 162 us
  blocking collectives: 76.9 us -> 0 us
  waiting for transfers between devices: 70.6 us -> 0 us
  starting transfers between devices: 5.18 us -> 0 us
    pallas_call x2 -> x1, Pallas kernels: 34.7 us -> 147 us  [body(): pl.pallas_call(functools.partial(exchange, shards), out_shape=jax.ShapeDt...]
    all_to_all x1 -> x0, blocking collectives: 76.9 us -> none  [body(): lax.all_to_all(back.reshape(shards, 2 * cols, rows_local), 'row', split_a...]
    all_to_all x1 -> x0, waiting for transfers between devices: 70.6 us -> none  [body(): lax.all_to_all(spectrum.reshape(shards, 2 * cols, rows_local), 'row', spl...]
    all_to_all x1 -> x0, starting transfers between devices: 5.18 us -> none  [body(): lax.all_to_all(spectrum.reshape(shards, 2 * cols, rows_local), 'row', spl...]
  transfers between devices with their start and end apart: 1 -> 0, of which waited for: 1 -> 0; matrix products, arithmetic and copies ran while one was open for 0% -> 0% of each run, Pallas kernels for 0% -> 0%
where the time goes in v2:
time: 164 us; the launch traced here: 163 us
  Pallas kernels  162 us (99%)
    pallas_call x1, Pallas kernels, body(): pl.pallas_call(functools.partial(exchange, shards), out_shape=jax.ShapeDt...  147 us
    pallas_call x1, Pallas kernels, body(): pl.pallas_call(rows_inverse, grid=(rows_local // block,), out_shape=jax.S...  14.6 us

profile of v2, /device:TPU:0, one launch (start us, length us, event | category | flops | bytes accessed | tf_op | source)
XLA Modules:
  0.0 162.5 jit_solution(11334414711626255579)
XLA Ops:
  0.7 147.3 %shard_map.91 = f32[8,3,2,64,512]{4,3,2,1,0:T(8,128)} custom-call(s32[1]{0:T(128)S(6)} %copy.10.cutoff_ref, f32[512,4096]{1,0:T(8,128)} %image_ref.3, bf16[2,2,1,384,512]{4,3,2,1,0:T(8,128)(2,1)} %constant.14.clone.row_ref, f32[2,16,256]{2,1,0:T(8,128)} %constant.15.clone.tw_ref, s32[8,3,64,128]{3,2,1,0:T(8,128)} %constant.16.clone.fx2_ref, ...), custom_call_target="tpu_custom_call" | custom-call | tf_op jit(solution)/shard_map/pallas_call | solution.py:395
  147.9 14.6 %shard_map.92 = f32[512,4096]{1,0:T(8,128)} custom-call(f32[8,384,512]{2,1,0:T(8,128)} %bitcast.1, f32[512,4096]{1,0:T(8,128)} %image_ref.3, bf16[2,2,384,512]{3,2,1,0:T(8,128)(2,1)} %constant.20.clone.table_ref, f32[2,16,256]{2,1,0:T(8,128)} %constant.15.clone.tw_ref), custom_call_target="tpu_custom_call" | custom-call | tf_op jit(solution)/shard_map/pallas_call | solution.py:419

commit v3 on v2

--- a/solution.py
+++ b/solution.py
@@ -136,7 +136,7 @@
     return forward0, forward, inverse0, inverse
 
 
-def rows_forward(image_ref, tw_ref, high_ref, low_ref):
+def rows_forward(image_ref, slab_copy, slabs, tw_ref, high_ref, low_ref):
     rows, length = image_ref.shape
     chunk = length // RADIX
     lanes = min(128, chunk)
@@ -161,7 +161,10 @@
                     low_ref[unit, at, part * chunk + start : part * chunk + start + lanes] = low
         return carry
 
-    lax.fori_loop(0, rows // sub, step, 0)
+    count = rows // sub // slabs
+    for slab in range(slabs):
+        slab_copy(slab).wait()
+        lax.fori_loop(slab * count, (slab + 1) * count, step, 0)
 
 
 def columns_filter(group, position, cutoff_ref, data_ref, fx2_ref, fy2_ref, fwd_ref, inv_ref, tw_ref, out_ref, work_ref):
@@ -234,8 +237,8 @@
 
 
 def exchange(
-    shards, cutoff_ref, image_ref, row_ref, tw_ref, fx2_ref, fy2_ref, fwd_ref, inv_ref, out_ref,
-    high_ref, low_ref, sent_ref, held_ref, work_ref, back_ref, send_sem, recv_sem, back_send, back_recv, own_sem,
+    shards, cutoff_ref, image_hbm, row_ref, tw_ref, fx2_ref, fy2_ref, fwd_ref, inv_ref, out_ref,
+    high_ref, low_ref, sent_ref, held_ref, work_ref, back_ref, send_sem, recv_sem, back_send, back_recv, own_sem, image_ref, slab_sem,
 ):
     groups, _, _, cols, rows = held_ref.shape
     per = shards // UNITS
@@ -276,13 +279,21 @@
 
         lax.fori_loop(1, shards, loop, 0)
 
+    slabs = slab_sem.shape[0]
+
+    def slab_copy(slab):
+        span = pl.ds(slab * (rows // slabs), rows // slabs)
+        return pltpu.make_async_copy(image_hbm.at[span], image_ref.at[span], slab_sem.at[slab])
+
+    for slab in range(slabs):
+        slab_copy(slab).start()
     barrier = pltpu.get_barrier_semaphore()
     every(
         lambda step: pl.semaphore_signal(
             barrier, inc=1, device_id={"row": partner(step)}, device_id_type=pl.DeviceIdType.MESH
         )
     )
-    rows_forward(image_ref, tw_ref, high_ref, low_ref)
+    rows_forward(image_ref, slab_copy, slabs, tw_ref, high_ref, low_ref)
     pl.semaphore_wait(barrier, shards - 1)
 
     def columns_of(dest):
@@ -331,11 +342,11 @@
     chunk = length // RADIX
     lanes = min(128, chunk)
     sub = 8
-    for unit in range(UNITS):
-        which = min(unit, 1)
-        work_ref[unit] = product(
-            split(data_ref[unit].T), (table_ref[which, 0], table_ref[which, 1]), (((1,), (0,)), ((), ()))
-        )
+    dims = (((1,), (0,)), ((), ()))
+    work_ref[0] = product(split(data_ref[0].T), (table_ref[0, 0], table_ref[0, 1]), dims)
+    rest = jnp.concatenate([data_ref[unit].T for unit in range(1, UNITS)], axis=0)
+    turned = product(split(rest), (table_ref[1, 0], table_ref[1, 1]), dims)
+    work_ref[1:] = turned.reshape(UNITS - 1, rows, 2 * chunk)
 
     def step(index, carry):
         at = pl.ds(pl.multiple_of(index * sub, sub), sub)
@@ -395,7 +406,7 @@
     returned = pl.pallas_call(
         functools.partial(exchange, shards),
         out_shape=jax.ShapeDtypeStruct((shards, groups, 2, part, rows_local), jnp.float32),
-        in_specs=[pl.BlockSpec(memory_space=pltpu.SMEM)] + [vmem] * 7,
+        in_specs=[pl.BlockSpec(memory_space=pltpu.SMEM), pl.BlockSpec(memory_space=pl.ANY)] + [vmem] * 6,
         out_specs=pl.BlockSpec(memory_space=pl.ANY),
         scratch_shapes=[
             pltpu.VMEM((UNITS, rows_local, 2 * chunk), jnp.bfloat16),
@@ -409,6 +420,8 @@
             pltpu.SemaphoreType.DMA((groups, shards)),
             pltpu.SemaphoreType.DMA((groups, shards)),
             pltpu.SemaphoreType.DMA((groups,)),
+            pltpu.VMEM((rows_local, width), jnp.float32),
+            pltpu.SemaphoreType.DMA((math.gcd(rows_local // 16, 4),)),
         ],
         compiler_params=pltpu.CompilerParams(
             vmem_limit_bytes=VMEM, collective_id=0, has_side_effects=True

time: 164 us -> 164 us (level)
  no operation moved by 1% of the time
where the time goes in v3:
time: 164 us; the launch traced here: 162 us
  Pallas kernels  161 us (98%)
    pallas_call x1, Pallas kernels, body(): pl.pallas_call(functools.partial(exchange, shards), out_shape=jax.ShapeDt...  147 us
    pallas_call x1, Pallas kernels, body(): pl.pallas_call(rows_inverse, grid=(rows_local // block,), out_shape=jax.S...  14.6 us

profile of v3, /device:TPU:0, one launch (start us, length us, event | category | flops | bytes accessed | tf_op | source)
XLA Modules:
  0.0 161.8 jit_solution(2461368318819532504)
XLA Ops:
  0.7 146.6 %shard_map.91 = f32[8,3,2,64,512]{4,3,2,1,0:T(8,128)} custom-call(s32[1]{0:T(128)S(6)} %copy.10.cutoff_ref, f32[512,4096]{1,0:T(8,128)} %image_ref.1, bf16[2,2,1,384,512]{4,3,2,1,0:T(8,128)(2,1)} %constant.14.clone.row_ref, f32[2,16,256]{2,1,0:T(8,128)} %constant.15.clone.tw_ref, s32[8,3,64,128]{3,2,1,0:T(8,128)} %constant.16.clone.fx2_ref, ...), custom_call_target="tpu_custom_call" | custom-call | tf_op jit(solution)/shard_map/pallas_call | solution.py:406
  147.3 14.6 %shard_map.92 = f32[512,4096]{1,0:T(8,128)} custom-call(f32[8,384,512]{2,1,0:T(8,128)} %bitcast.1, f32[512,4096]{1,0:T(8,128)} %image_ref.1, bf16[2,2,384,512]{3,2,1,0:T(8,128)(2,1)} %constant.20.clone.table_ref, f32[2,16,256]{2,1,0:T(8,128)} %constant.15.clone.tw_ref), custom_call_target="tpu_custom_call" | custom-call | tf_op jit(solution)/shard_map/pallas_call | solution.py:432
